TPU v7x, 512 devices: a whole 4x4x16 slice. The times are simulated.
512 devices in a mesh: chan: 64 (over y, z_lo, core), tmpl: 8 (over x, z_hi).
Axes of the slice: x: 4, y: 4, z: 16 (z_hi: 2, z_lo: 8; z = z_hi * 8 + z_lo), core: 2. Of those that a mesh axis runs over, the one named last changes fastest.
Arguments:
- raw_stretches: bfloat16 [4096, 2, 8192], P('chan', None, 'tmpl'), may hold values from -500 to 500
- stretch_ids: int32 [4096], P('chan'), may hold values from -1 to 2047, as said below
- templates: bfloat16 [64, 8, 512, 256], P('chan', 'tmpl'), may hold values from -500 to 500
- offsets: int32 [64, 8], P('chan', 'tmpl'), may hold values from 0 to 63
Outputs:
- detection: float32 [64, 8, 8192], P('chan', None, 'tmpl')
Inputs may be any that keep to these rules, and one draw needn't show every extreme that they name: `stretch_ids`: the slots of ingest device i are rows i * 64 to i * 64 + 63. Its stretches fill its first slots in increasing order of stretch id, the rest are -1. Every stretch id appears exactly once; stretch p belongs to channel group p // 32. No ingest device holds two stretches of one channel group, and one ingest device holds a stretch of every channel group.
All inputs are finite; a program needn't handle non-finite values.
Results may differ from a plain program's by a relative error of at most 0.0003.
Values may be sent and summed in bfloat16 or wider, within the bound.
A program may use at most 192 MiB of HBM per device.

v0:
```python
from functools import partial

import jax
import jax.numpy as jnp
from jax import lax
from jax.sharding import PartitionSpec as P


def shifted(value, axis, steps):
    count = lax.axis_size(axis)
    leading, last = (max(0, -steps), min(count, count - steps))
    return lax.ppermute(value, axis, [(source, source + steps) for source in range(leading, last)])


def passed_along(value, axis, steps):
    count = lax.axis_size(axis)
    pairs = [(source, (source + steps) % count) for source in range(count)]
    return lax.ppermute(value, axis, pairs)


def diagonal_sums(products, length):
    count, taps, columns = products.shape
    flattened = jnp.pad(products.reshape(count, taps * columns), ((0, 0), (0, taps)))
    skewed = flattened.reshape(count, taps, columns + 1)[:, :, :length]
    return jnp.sum(skewed, axis=1)


def band_matrix(columns, length, taps):
    upper = lax.broadcasted_iota(jnp.int32, (columns, length), 0)
    lower = lax.broadcasted_iota(jnp.int32, (columns, length), 1)
    spread = upper - lower
    return ((spread >= 0) & (spread < taps)).astype(jnp.float32)


def row_masks(begins, total_rows, span_rows):
    rows_iota = lax.broadcasted_iota(jnp.int32, (begins.shape[0], total_rows), 1)
    inside = (rows_iota >= begins[:, None]) & (rows_iota < begins[:, None] + span_rows)
    return inside.astype(jnp.float32)


def take_rows(source, begin_row, count):
    return lax.dynamic_slice_in_dim(source, begin_row, count, 0)


def body(raw_stretches, stretch_ids, templates, offsets):
    group_count = lax.axis_size("chan")
    stop_count = lax.axis_size("tmpl")
    slot_count, stretch_width, segment = raw_stretches.shape
    per_group = group_count // 2
    group_rows = per_group * stretch_width
    block_size = templates.shape[1]
    span_rows = templates.shape[2]
    taps = templates.shape[3]
    reach = span_rows // group_rows
    homed = block_size * stop_count
    volume = float(span_rows * taps)
    owners = jnp.where(stretch_ids >= 0, stretch_ids // per_group, -1)
    dest_iota = lax.broadcasted_iota(jnp.int32, (group_count, slot_count), 0)
    select = owners[None, :] == dest_iota
    outgoing = jnp.dot(
        select.astype(jnp.bfloat16),
        raw_stretches.reshape(slot_count, stretch_width * segment),
        preferred_element_type=jnp.float32,
    )
    outgoing = outgoing.astype(jnp.bfloat16).reshape(group_count, stretch_width, segment)
    places = jnp.sum(jnp.where(select, stretch_ids[None, :] % per_group + 1, 0), axis=1) - 1
    arrived, arrived_places = (
        lax.all_to_all(outgoing, "chan", split_axis=0, concat_axis=0, tiled=True),
        lax.all_to_all(places, "chan", split_axis=0, concat_axis=0, tiled=True),
    )
    place_iota = lax.broadcasted_iota(jnp.int32, (per_group, group_count), 0)
    pick = (arrived_places[None, :] == place_iota).astype(jnp.bfloat16)
    local = jnp.dot(
        pick,
        arrived.reshape(group_count, stretch_width * segment),
        preferred_element_type=jnp.float32,
    )
    local = local.astype(jnp.bfloat16).reshape(group_rows, segment)
    following = shifted(local[:, :taps], "tmpl", -1)
    record = jnp.concatenate([local, following], axis=1)
    band = band_matrix(segment + taps, segment, taps)
    stacked = [record]
    for level in range(1, reach + 1):
        stacked.append(shifted(record, "chan", -level))
    extended = jnp.concatenate(stacked, axis=0)
    squares = jnp.square(extended.astype(jnp.float32))
    sliding = jnp.dot(squares, band, precision=lax.Precision.HIGHEST)
    numer_total = jnp.zeros((homed, segment), jnp.float32)
    energy_total = jnp.zeros((homed, segment), jnp.float32)
    norms = jnp.zeros((homed,), jnp.float32)
    block_now = templates[0]
    shift_now = offsets[0]
    for stop_step in range(stop_count):
        if stop_step > 0:
            block_now, shift_now = passed_along((block_now, shift_now), "tmpl", 1)
        block_index = (lax.axis_index("tmpl") - stop_step) % stop_count
        first_row = block_index * block_size
        block_norms = jnp.sum(jnp.square(block_now.astype(jnp.float32)), axis=(1, 2))
        norms = lax.dynamic_update_slice(norms, block_norms, (first_row,))
        window_rows = jax.vmap(partial(take_rows, count=span_rows), in_axes=(None, 0))(
            extended, shift_now
        )
        products = jnp.einsum(
            "kql,kqw->klw", block_now, window_rows, preferred_element_type=jnp.float32
        )
        numer = diagonal_sums(products, segment)
        masks = row_masks(shift_now, extended.shape[0], span_rows)
        energy = jnp.dot(masks, sliding, precision=lax.Precision.HIGHEST)
        numer_total = lax.dynamic_update_slice(numer_total, numer, (first_row, 0))
        energy_total = lax.dynamic_update_slice(energy_total, energy, (first_row, 0))
    detection = numer_total * jnp.sqrt(
        volume / (jnp.maximum(energy_total, volume) * norms[:, None])
    )
    return detection.reshape(1, homed, segment)


def solution(mesh):
    placed = (P("chan", None, "tmpl"), P("chan"), P("chan", "tmpl", None, None), P("chan", "tmpl"))
    return jax.shard_map(
        body, mesh=mesh, in_specs=placed, out_specs=P("chan", None, "tmpl"), check_vma=False
    )
```

profile of v0, /device:TPU:77, one launch (start us, length us, event | category | flops | bytes accessed | tf_op | source)
XLA Modules:
  0.0 588.4 jit_solution(13918209871166426284)
XLA Ops:
  1.5 15.6 %all-to-all-start = ((s32[64,1,1]{2,1,0:T(1,128)}), s32[64,1,1]{2,1,0:T(1,128)S(1)}, u32[]{:S(2)}, u32[]{:S(2)}) async-start(s32[64,1,1]{2,1,0:T(1,128)} %copy.31), calls=%async_computation | async-start | bytes 65536 | tf_op jit(solution)/shard_map/all_to_all | solution.py:69
  17.1 7.9 %collective-permute-start.9 = (s32[1]{0:T(128)}, s32[1]{0:T(128)}, u32[]{:S(2)}, u32[]{:S(2)}) collective-permute-start(s32[1]{0:T(128)} %bitcast.1), channel_id=1, source_target_pairs={{0,1},{1,2},{2,3},{3,4},{4,5},{5,6},{6,7},{7,0},{8,9},{9,10},{10,1... | collective-permute-start | bytes 20 | tf_op jit(solution)/shard_map/ppermute | solution.py:18
  25.0 6.7 %collective-permute-start.10 = (bf16[1,512,256]{2,1,0:T(8,128)(2,1)}, bf16[1,512,256]{2,1,0:T(8,128)(2,1)S(1)}, u32[]{:S(2)}, u32[]{:S(2)}) collective-permute-start(bf16[1,512,256]{2,1,0:T(8,128)(2,1)} %bitcast.161), channel_id=1, source_target_pairs={{0,1},{1,2},{2,3},{3,4},{4,5},{5,6},{6,7},{7,0},{8,9},{9,10},{10,1... | collective-permute-start | bytes 786440 | tf_op jit(solution)/shard_map/ppermute | solution.py:18
  37.7 13.6 %all-to-all-start.1 = ((bf16[64,2,1024]{2,1,0:T(2,128)(2,1)}), bf16[64,2,1024]{2,1,0:T(2,128)(2,1)S(1)}, u32[]{:S(2)}, u32[]{:S(2)}) async-start(bf16[64,2,1024]{2,1,0:T(2,128)(2,1)} %reshape.355), calls=%async_computation.1 | async-start | bytes 524288 | tf_op jit(solution)/shard_map/all_to_all | solution.py:68
  52.0 7.9 %collective-permute-start.11 = (s32[1]{0:T(128)}, s32[1]{0:T(128)}, u32[]{:S(2)}, u32[]{:S(2)}) collective-permute-start(s32[1]{0:T(128)} %collective-permute-done.9), channel_id=1, source_target_pairs={{0,1},{1,2},{2,3},{3,4},{4,5},{5,6},{6,7},{7,0},{8,9},{9,10},{10,1... | collective-permute-start | bytes 20 | tf_op jit(solution)/shard_map/ppermute | solution.py:18
  61.8 14.2 %collective-permute-done.11 = s32[1]{0:T(128)} collective-permute-done((s32[1]{0:T(128)}, s32[1]{0:T(128)}, u32[]{:S(2)}, u32[]{:S(2)}) %collective-permute-start.11) | collective-permute-done | bytes 36 | tf_op jit(solution)/shard_map/ppermute | solution.py:18
  77.1 7.7 %collective-permute-start.13 = (s32[1]{0:T(128)}, s32[1]{0:T(128)}, u32[]{:S(2)}, u32[]{:S(2)}) collective-permute-start(s32[1]{0:T(128)} %collective-permute-done.11), channel_id=1, source_target_pairs={{0,1},{1,2},{2,3},{3,4},{4,5},{5,6},{6,7},{7,0},{8,9},{9,10},{10,1... | collective-permute-start | bytes 20 | tf_op jit(solution)/shard_map/ppermute | solution.py:18
  92.6 6.8 %collective-permute-start.15 = (s32[1]{0:T(128)}, s32[1]{0:T(128)}, u32[]{:S(2)}, u32[]{:S(2)}) collective-permute-start(s32[1]{0:T(128)} %collective-permute-done.13), channel_id=1, source_target_pairs={{0,1},{1,2},{2,3},{3,4},{4,5},{5,6},{6,7},{7,0},{8,9},{9,10},{10,1... | collective-permute-start | bytes 20 | tf_op jit(solution)/shard_map/ppermute | solution.py:18
  114.0 8.8 %collective-permute-start.17 = (s32[1]{0:T(128)}, s32[1]{0:T(128)}, u32[]{:S(2)}, u32[]{:S(2)}) collective-permute-start(s32[1]{0:T(128)} %collective-permute-done.15), channel_id=1, source_target_pairs={{0,1},{1,2},{2,3},{3,4},{4,5},{5,6},{6,7},{7,0},{8,9},{9,10},{10,1... | collective-permute-start | bytes 20 | tf_op jit(solution)/shard_map/ppermute | solution.py:18
  124.7 11.9 %collective-permute-done.17 = s32[1]{0:T(128)} collective-permute-done((s32[1]{0:T(128)}, s32[1]{0:T(128)}, u32[]{:S(2)}, u32[]{:S(2)}) %collective-permute-start.17) | collective-permute-done | bytes 36 | tf_op jit(solution)/shard_map/ppermute | solution.py:18
  138.1 6.9 %collective-permute-start.19 = (s32[1]{0:T(128)}, s32[1]{0:T(128)}, u32[]{:S(2)}, u32[]{:S(2)}) collective-permute-start(s32[1]{0:T(128)} %collective-permute-done.17), channel_id=1, source_target_pairs={{0,1},{1,2},{2,3},{3,4},{4,5},{5,6},{6,7},{7,0},{8,9},{9,10},{10,1... | collective-permute-start | bytes 20 | tf_op jit(solution)/shard_map/ppermute | solution.py:18
  161.0 6.3 %collective-permute-done.21 = s32[1]{0:T(128)} collective-permute-done((s32[1]{0:T(128)}, s32[1]{0:T(128)}, u32[]{:S(2)}, u32[]{:S(2)}) %collective-permute-start.21) | collective-permute-done | bytes 36 | tf_op jit(solution)/shard_map/ppermute | solution.py:18
  179.8 17.3 %collective-permute-done.14 = bf16[1,512,256]{2,1,0:T(8,128)(2,1)S(1)} collective-permute-done((bf16[1,512,256]{2,1,0:T(8,128)(2,1)S(1)}, bf16[1,512,256]{2,1,0:T(8,128)(2,1)S(1)}, u32[]{:S(2)}, u32[]{:S(2)}) %collective-permute-start.14) | collective-permute-done | bytes 262176 | tf_op jit(solution)/shard_map/ppermute | solution.py:18
  201.3 11.0 %collective-permute-start = (bf16[64,256]{1,0:T(8,128)(2,1)S(1)}, bf16[64,256]{1,0:T(8,128)(2,1)S(1)}, u32[]{:S(2)}, u32[]{:S(2)}) collective-permute-start(bf16[64,256]{1,0:T(8,128)(2,1)S(1)} %slice.132), channel_id=1, source_target_pairs={{1,0},{2,1},{3,2},{4,3},{5,4},{6,5},{7,6},{9,8},{10,9},{11,10},{12... | collective-permute-start | bytes 98312 | tf_op jit(solution)/shard_map/ppermute | solution.py:12
  213.0 6.1 %collective-permute-done = bf16[64,256]{1,0:T(8,128)(2,1)S(1)} collective-permute-done((bf16[64,256]{1,0:T(8,128)(2,1)S(1)}, bf16[64,256]{1,0:T(8,128)(2,1)S(1)}, u32[]{:S(2)}, u32[]{:S(2)}) %collective-permute-start) | collective-permute-done | bytes 32800 | tf_op jit(solution)/shard_map/ppermute | solution.py:12
  225.4 6.0 %collective-permute-start.18 = (bf16[1,512,256]{2,1,0:T(8,128)(2,1)S(1)}, bf16[1,512,256]{2,1,0:T(8,128)(2,1)S(1)}, u32[]{:S(2)}, u32[]{:S(2)}) collective-permute-start(bf16[1,512,256]{2,1,0:T(8,128)(2,1)S(1)} %collective-permute-done.16), channel_id=1, source_target_pairs={{0,1},{1,2},{2,3},{3,4},{4,5},{5,6},{6,7},{7,0},{8,9},{9,10},{10,1... | collective-permute-start | bytes 786440 | tf_op jit(solution)/shard_map/ppermute | solution.py:18
  233.3 17.2 %collective-permute-start.3 = (bf16[64,1280]{1,0:T(8,128)(2,1)S(1)}, bf16[64,1280]{1,0:T(8,128)(2,1)S(1)}, u32[]{:S(2)}, u32[]{:S(2)}) collective-permute-start(bf16[64,1280]{1,0:T(8,128)(2,1)S(1)} %get-tuple-element.95), channel_id=1, source_target_pairs={{24,0},{32,8},{40,16},{48,24},{56,32},{64,40},{72,48},{80,56},{88,... | collective-permute-start | bytes 491528 | tf_op jit(solution)/shard_map/ppermute | solution.py:12
  255.1 16.8 %collective-permute-start.6 = (bf16[64,1280]{1,0:T(8,128)(2,1)S(1)}, bf16[64,1280]{1,0:T(8,128)(2,1)S(1)}, u32[]{:S(2)}, u32[]{:S(2)}) collective-permute-start(bf16[64,1280]{1,0:T(8,128)(2,1)S(1)} %get-tuple-element.95), channel_id=1, source_target_pairs={{48,0},{56,8},{64,16},{72,24},{80,32},{88,40},{96,48},{104,56},{11... | collective-permute-start | bytes 491528 | tf_op jit(solution)/shard_map/ppermute | solution.py:12
  282.4 23.6 %collective-permute-done.6 = bf16[64,1280]{1,0:T(8,128)(2,1)S(1)} collective-permute-done((bf16[64,1280]{1,0:T(8,128)(2,1)S(1)}, bf16[64,1280]{1,0:T(8,128)(2,1)S(1)}, u32[]{:S(2)}, u32[]{:S(2)}) %collective-permute-start.6) | collective-permute-done | bytes 163872 | tf_op jit(solution)/shard_map/ppermute | solution.py:12
  313.7 6.2 %fusion.3 = f32[576,1024]{1,0:T(8,128)S(1)} fusion(bf16[576,1280]{1,0:T(8,128)(2,1)} %constant_dynamic-update-slice_fusion.2), kind=kOutput, calls=%fused_computation.4 | convolution fusion | flops 9066414080 | bytes 3833856 | tf_op jit(solution)/shard_map/dot_general | solution.py:87
  334.7 14.6 %pad_reduce_fusion.7 = f32[327936]{0:T(1024)} fusion(f32[1,327680]{1,0:T(1,128)S(1)} %bitcast.146), kind=kLoop, calls=%fused_computation.26 | loop fusion | bytes 2622464 | tf_op jit(solution)/shard_map/jit(_pad)/pad | solution.py:23
  362.5 14.6 %pad_reduce_fusion.6 = f32[327936]{0:T(1024)} fusion(f32[1,327680]{1,0:T(1,128)S(1)} %bitcast.148), kind=kLoop, calls=%fused_computation.25 | loop fusion | bytes 2622464 | tf_op jit(solution)/shard_map/jit(_pad)/pad | solution.py:23
  390.4 14.6 %pad_reduce_fusion.5 = f32[327936]{0:T(1024)} fusion(f32[1,327680]{1,0:T(1,128)S(1)} %bitcast.150), kind=kLoop, calls=%fused_computation.24 | loop fusion | bytes 2622464 | tf_op jit(solution)/shard_map/jit(_pad)/pad | solution.py:23
  418.3 14.8 %pad_reduce_fusion.4 = f32[327936]{0:T(1024)} fusion(f32[1,327680]{1,0:T(1,128)S(1)} %bitcast.152), kind=kLoop, calls=%fused_computation.23 | loop fusion | bytes 2622464 | tf_op jit(solution)/shard_map/jit(_pad)/pad | solution.py:23
  446.3 14.6 %pad_reduce_fusion.3 = f32[327936]{0:T(1024)} fusion(f32[1,327680]{1,0:T(1,128)S(1)} %bitcast.154), kind=kLoop, calls=%fused_computation.22 | loop fusion | bytes 2622464 | tf_op jit(solution)/shard_map/jit(_pad)/pad | solution.py:23
  471.7 13.5 %pad_reduce_fusion.2 = f32[327936]{0:T(1024)S(1)} fusion(f32[1,327680]{1,0:T(1,128)S(1)} %bitcast.156), kind=kLoop, calls=%fused_computation.21 | loop fusion | bytes 2622464 | tf_op jit(solution)/shard_map/jit(_pad)/pad | solution.py:23
  486.4 9.1 %collective-permute-start.20 = (bf16[1,512,256]{2,1,0:T(8,128)(2,1)S(1)}, bf16[1,512,256]{2,1,0:T(8,128)(2,1)S(1)}, u32[]{:S(2)}, u32[]{:S(2)}) collective-permute-start(bf16[1,512,256]{2,1,0:T(8,128)(2,1)S(1)} %collective-permute-done.18), channel_id=1, source_target_pairs={{0,1},{1,2},{2,3},{3,4},{4,5},{5,6},{6,7},{7,0},{8,9},{9,10},{10,1... | collective-permute-start | bytes 786440 | tf_op jit(solution)/shard_map/ppermute | solution.py:18
  497.6 22.7 %collective-permute-done.20 = bf16[1,512,256]{2,1,0:T(8,128)(2,1)S(1)} collective-permute-done((bf16[1,512,256]{2,1,0:T(8,128)(2,1)S(1)}, bf16[1,512,256]{2,1,0:T(8,128)(2,1)S(1)}, u32[]{:S(2)}, u32[]{:S(2)}) %collective-permute-start.20) | collective-permute-done | bytes 262176 | tf_op jit(solution)/shard_map/ppermute | solution.py:18
  523.9 13.5 %pad_reduce_fusion.1 = f32[327936]{0:T(1024)S(1)} fusion(f32[1,327680]{1,0:T(1,128)S(1)} %bitcast.158), kind=kLoop, calls=%fused_computation.20 | loop fusion | bytes 2622464 | tf_op jit(solution)/shard_map/jit(_pad)/pad | solution.py:23
  538.6 6.9 %collective-permute-start.22 = (bf16[1,512,256]{2,1,0:T(8,128)(2,1)S(1)}, bf16[1,512,256]{2,1,0:T(8,128)(2,1)S(1)}, u32[]{:S(2)}, u32[]{:S(2)}) collective-permute-start(bf16[1,512,256]{2,1,0:T(8,128)(2,1)S(1)} %collective-permute-done.20), channel_id=1, source_target_pairs={{0,1},{1,2},{2,3},{3,4},{4,5},{5,6},{6,7},{7,0},{8,9},{9,10},{10,1... | collective-permute-start | bytes 786440 | tf_op jit(solution)/shard_map/ppermute | solution.py:18
  547.3 20.2 %collective-permute-done.22 = bf16[1,512,256]{2,1,0:T(8,128)(2,1)S(1)} collective-permute-done((bf16[1,512,256]{2,1,0:T(8,128)(2,1)S(1)}, bf16[1,512,256]{2,1,0:T(8,128)(2,1)S(1)}, u32[]{:S(2)}, u32[]{:S(2)}) %collective-permute-start.22) | collective-permute-done | bytes 262176 | tf_op jit(solution)/shard_map/ppermute | solution.py:18
  571.1 13.5 %pad_reduce_fusion = f32[327936]{0:T(1024)S(1)} fusion(f32[1,327680]{1,0:T(1,128)S(1)} %bitcast.160), kind=kLoop, calls=%fused_computation.19 | loop fusion | bytes 2622464 | tf_op jit(solution)/shard_map/jit(_pad)/pad | solution.py:23
  (155 shorter events, 177.6 us)
Async XLA Ops:
  1.5 36.2 %all-to-all-start = ((s32[64,1,1]{2,1,0:T(1,128)}), s32[64,1,1]{2,1,0:T(1,128)S(1)}, u32[]{:S(2)}, u32[]{:S(2)}) async-start(s32[64,1,1]{2,1,0:T(1,128)} %copy.31), calls=%async_computation | async-start | bytes 65536 | tf_op jit(solution)/shard_map/all_to_all | solution.py:69
  17.1 19.9 %collective-permute-start.9 = (s32[1]{0:T(128)}, s32[1]{0:T(128)}, u32[]{:S(2)}, u32[]{:S(2)}) collective-permute-start(s32[1]{0:T(128)} %bitcast.1), channel_id=1, source_target_pairs={{0,1},{1,2},{2,3},{3,4},{4,5},{5,6},{6,7},{7,0},{8,9},{9,10},{10,1... | collective-permute-start | bytes 20 | tf_op jit(solution)/shard_map/ppermute | solution.py:18
  25.0 82.4 %collective-permute-start.10 = (bf16[1,512,256]{2,1,0:T(8,128)(2,1)}, bf16[1,512,256]{2,1,0:T(8,128)(2,1)S(1)}, u32[]{:S(2)}, u32[]{:S(2)}) collective-permute-start(bf16[1,512,256]{2,1,0:T(8,128)(2,1)} %bitcast.161), channel_id=1, source_target_pairs={{0,1},{1,2},{2,3},{3,4},{4,5},{5,6},{6,7},{7,0},{8,9},{9,10},{10,1... | collective-permute-start | bytes 786440 | tf_op jit(solution)/shard_map/ppermute | solution.py:18
  37.7 163.3 %all-to-all-start.1 = ((bf16[64,2,1024]{2,1,0:T(2,128)(2,1)}), bf16[64,2,1024]{2,1,0:T(2,128)(2,1)S(1)}, u32[]{:S(2)}, u32[]{:S(2)}) async-start(bf16[64,2,1024]{2,1,0:T(2,128)(2,1)} %reshape.355), calls=%async_computation.1 | async-start | bytes 524288 | tf_op jit(solution)/shard_map/all_to_all | solution.py:68
  52.0 24.0 %collective-permute-start.11 = (s32[1]{0:T(128)}, s32[1]{0:T(128)}, u32[]{:S(2)}, u32[]{:S(2)}) collective-permute-start(s32[1]{0:T(128)} %collective-permute-done.9), channel_id=1, source_target_pairs={{0,1},{1,2},{2,3},{3,4},{4,5},{5,6},{6,7},{7,0},{8,9},{9,10},{10,1... | collective-permute-start | bytes 20 | tf_op jit(solution)/shard_map/ppermute | solution.py:18
  77.1 14.1 %collective-permute-start.13 = (s32[1]{0:T(128)}, s32[1]{0:T(128)}, u32[]{:S(2)}, u32[]{:S(2)}) collective-permute-start(s32[1]{0:T(128)} %collective-permute-done.11), channel_id=1, source_target_pairs={{0,1},{1,2},{2,3},{3,4},{4,5},{5,6},{6,7},{7,0},{8,9},{9,10},{10,1... | collective-permute-start | bytes 20 | tf_op jit(solution)/shard_map/ppermute | solution.py:18
  92.6 14.2 %collective-permute-start.15 = (s32[1]{0:T(128)}, s32[1]{0:T(128)}, u32[]{:S(2)}, u32[]{:S(2)}) collective-permute-start(s32[1]{0:T(128)} %collective-permute-done.13), channel_id=1, source_target_pairs={{0,1},{1,2},{2,3},{3,4},{4,5},{5,6},{6,7},{7,0},{8,9},{9,10},{10,1... | collective-permute-start | bytes 20 | tf_op jit(solution)/shard_map/ppermute | solution.py:18
  107.5 60.5 %collective-permute-start.12 = (bf16[1,512,256]{2,1,0:T(8,128)(2,1)S(1)}, bf16[1,512,256]{2,1,0:T(8,128)(2,1)S(1)}, u32[]{:S(2)}, u32[]{:S(2)}) collective-permute-start(bf16[1,512,256]{2,1,0:T(8,128)(2,1)S(1)} %collective-permute-done.10), channel_id=1, source_target_pairs={{0,1},{1,2},{2,3},{3,4},{4,5},{5,6},{6,7},{7,0},{8,9},{9,10},{10,1... | collective-permute-start | bytes 786440 | tf_op jit(solution)/shard_map/ppermute | solution.py:18
  114.0 22.6 %collective-permute-start.17 = (s32[1]{0:T(128)}, s32[1]{0:T(128)}, u32[]{:S(2)}, u32[]{:S(2)}) collective-permute-start(s32[1]{0:T(128)} %collective-permute-done.15), channel_id=1, source_target_pairs={{0,1},{1,2},{2,3},{3,4},{4,5},{5,6},{6,7},{7,0},{8,9},{9,10},{10,1... | collective-permute-start | bytes 20 | tf_op jit(solution)/shard_map/ppermute | solution.py:18
  138.1 14.1 %collective-permute-start.19 = (s32[1]{0:T(128)}, s32[1]{0:T(128)}, u32[]{:S(2)}, u32[]{:S(2)}) collective-permute-start(s32[1]{0:T(128)} %collective-permute-done.17), channel_id=1, source_target_pairs={{0,1},{1,2},{2,3},{3,4},{4,5},{5,6},{6,7},{7,0},{8,9},{9,10},{10,1... | collective-permute-start | bytes 20 | tf_op jit(solution)/shard_map/ppermute | solution.py:18
  153.3 14.1 %collective-permute-start.21 = (s32[1]{0:T(128)}, s32[1]{0:T(128)}, u32[]{:S(2)}, u32[]{:S(2)}) collective-permute-start(s32[1]{0:T(128)} %collective-permute-done.19), channel_id=1, source_target_pairs={{0,1},{1,2},{2,3},{3,4},{4,5},{5,6},{6,7},{7,0},{8,9},{9,10},{10,1... | collective-permute-start | bytes 20 | tf_op jit(solution)/shard_map/ppermute | solution.py:18
  168.0 29.1 %collective-permute-start.14 = (bf16[1,512,256]{2,1,0:T(8,128)(2,1)S(1)}, bf16[1,512,256]{2,1,0:T(8,128)(2,1)S(1)}, u32[]{:S(2)}, u32[]{:S(2)}) collective-permute-start(bf16[1,512,256]{2,1,0:T(8,128)(2,1)S(1)} %collective-permute-done.12), channel_id=1, source_target_pairs={{0,1},{1,2},{2,3},{3,4},{4,5},{5,6},{6,7},{7,0},{8,9},{9,10},{10,1... | collective-permute-start | bytes 786440 | tf_op jit(solution)/shard_map/ppermute | solution.py:18
  197.2 75.4 %copy-start.1 = (bf16[1,512,256]{2,1,0:T(8,128)(2,1)}, bf16[1,512,256]{2,1,0:T(8,128)(2,1)S(1)}, u32[]{:S(2)}) copy-start(bf16[1,512,256]{2,1,0:T(8,128)(2,1)S(1)} %collective-permute-done.14) | copy-start | bytes 786436
  197.2 26.7 %collective-permute-start.16 = (bf16[1,512,256]{2,1,0:T(8,128)(2,1)S(1)}, bf16[1,512,256]{2,1,0:T(8,128)(2,1)S(1)}, u32[]{:S(2)}, u32[]{:S(2)}) collective-permute-start(bf16[1,512,256]{2,1,0:T(8,128)(2,1)S(1)} %collective-permute-done.14), channel_id=1, source_target_pairs={{0,1},{1,2},{2,3},{3,4},{4,5},{5,6},{6,7},{7,0},{8,9},{9,10},{10,1... | collective-permute-start | bytes 786440 | tf_op jit(solution)/shard_map/ppermute | solution.py:18
  201.3 17.8 %collective-permute-start = (bf16[64,256]{1,0:T(8,128)(2,1)S(1)}, bf16[64,256]{1,0:T(8,128)(2,1)S(1)}, u32[]{:S(2)}, u32[]{:S(2)}) collective-permute-start(bf16[64,256]{1,0:T(8,128)(2,1)S(1)} %slice.132), channel_id=1, source_target_pairs={{1,0},{2,1},{3,2},{4,3},{5,4},{6,5},{7,6},{9,8},{10,9},{11,10},{12... | collective-permute-start | bytes 98312 | tf_op jit(solution)/shard_map/ppermute | solution.py:12
  219.8 32.7 %collective-permute-start.1 = (bf16[64,1280]{1,0:T(8,128)(2,1)S(1)}, bf16[64,1280]{1,0:T(8,128)(2,1)S(1)}, u32[]{:S(2)}, u32[]{:S(2)}) collective-permute-start(bf16[64,1280]{1,0:T(8,128)(2,1)S(1)} %get-tuple-element.95), channel_id=1, source_target_pairs={{8,0},{16,8},{24,16},{32,24},{40,32},{48,40},{56,48},{64,56},{72,6... | collective-permute-start | bytes 491528 | tf_op jit(solution)/shard_map/ppermute | solution.py:12
  225.4 242.7 %collective-permute-start.18 = (bf16[1,512,256]{2,1,0:T(8,128)(2,1)S(1)}, bf16[1,512,256]{2,1,0:T(8,128)(2,1)S(1)}, u32[]{:S(2)}, u32[]{:S(2)}) collective-permute-start(bf16[1,512,256]{2,1,0:T(8,128)(2,1)S(1)} %collective-permute-done.16), channel_id=1, source_target_pairs={{0,1},{1,2},{2,3},{3,4},{4,5},{5,6},{6,7},{7,0},{8,9},{9,10},{10,1... | collective-permute-start | bytes 786440 | tf_op jit(solution)/shard_map/ppermute | solution.py:18
  231.4 23.7 %collective-permute-start.2 = (bf16[64,1280]{1,0:T(8,128)(2,1)S(1)}, bf16[64,1280]{1,0:T(8,128)(2,1)S(1)}, u32[]{:S(2)}, u32[]{:S(2)}) collective-permute-start(bf16[64,1280]{1,0:T(8,128)(2,1)S(1)} %get-tuple-element.95), channel_id=1, source_target_pairs={{16,0},{24,8},{32,16},{40,24},{48,32},{56,40},{64,48},{72,56},{80,... | collective-permute-start | bytes 491528 | tf_op jit(solution)/shard_map/ppermute | solution.py:12
  233.3 39.2 %collective-permute-start.3 = (bf16[64,1280]{1,0:T(8,128)(2,1)S(1)}, bf16[64,1280]{1,0:T(8,128)(2,1)S(1)}, u32[]{:S(2)}, u32[]{:S(2)}) collective-permute-start(bf16[64,1280]{1,0:T(8,128)(2,1)S(1)} %get-tuple-element.95), channel_id=1, source_target_pairs={{24,0},{32,8},{40,16},{48,24},{56,32},{64,40},{72,48},{80,56},{88,... | collective-permute-start | bytes 491528 | tf_op jit(solution)/shard_map/ppermute | solution.py:12
  250.5 25.9 %collective-permute-start.4 = (bf16[64,1280]{1,0:T(8,128)(2,1)S(1)}, bf16[64,1280]{1,0:T(8,128)(2,1)S(1)}, u32[]{:S(2)}, u32[]{:S(2)}) collective-permute-start(bf16[64,1280]{1,0:T(8,128)(2,1)S(1)} %get-tuple-element.95), channel_id=1, source_target_pairs={{32,0},{40,8},{48,16},{56,24},{64,32},{72,40},{80,48},{88,56},{96,... | collective-permute-start | bytes 491528 | tf_op jit(solution)/shard_map/ppermute | solution.py:12
  252.5 29.3 %collective-permute-start.5 = (bf16[64,1280]{1,0:T(8,128)(2,1)S(1)}, bf16[64,1280]{1,0:T(8,128)(2,1)S(1)}, u32[]{:S(2)}, u32[]{:S(2)}) collective-permute-start(bf16[64,1280]{1,0:T(8,128)(2,1)S(1)} %get-tuple-element.95), channel_id=1, source_target_pairs={{40,0},{48,8},{56,16},{64,24},{72,32},{80,40},{88,48},{96,56},{104... | collective-permute-start | bytes 491528 | tf_op jit(solution)/shard_map/ppermute | solution.py:12
  255.1 51.0 %collective-permute-start.6 = (bf16[64,1280]{1,0:T(8,128)(2,1)S(1)}, bf16[64,1280]{1,0:T(8,128)(2,1)S(1)}, u32[]{:S(2)}, u32[]{:S(2)}) collective-permute-start(bf16[64,1280]{1,0:T(8,128)(2,1)S(1)} %get-tuple-element.95), channel_id=1, source_target_pairs={{48,0},{56,8},{64,16},{72,24},{80,32},{88,40},{96,48},{104,56},{11... | collective-permute-start | bytes 491528 | tf_op jit(solution)/shard_map/ppermute | solution.py:12
  272.5 37.0 %collective-permute-start.7 = (bf16[64,1280]{1,0:T(8,128)(2,1)S(1)}, bf16[64,1280]{1,0:T(8,128)(2,1)S(1)}, u32[]{:S(2)}, u32[]{:S(2)}) collective-permute-start(bf16[64,1280]{1,0:T(8,128)(2,1)S(1)} %get-tuple-element.95), channel_id=1, source_target_pairs={{56,0},{64,8},{72,16},{80,24},{88,32},{96,40},{104,48},{112,56},{1... | collective-permute-start | bytes 491528 | tf_op jit(solution)/shard_map/ppermute | solution.py:12
  276.5 36.6 %collective-permute-start.8 = (bf16[64,1280]{1,0:T(8,128)(2,1)S(1)}, bf16[64,1280]{1,0:T(8,128)(2,1)S(1)}, u32[]{:S(2)}, u32[]{:S(2)}) collective-permute-start(bf16[64,1280]{1,0:T(8,128)(2,1)S(1)} %get-tuple-element.95), channel_id=1, source_target_pairs={{64,0},{72,8},{80,16},{88,24},{96,32},{104,40},{112,48},{120,56},{... | collective-permute-start | bytes 491528 | tf_op jit(solution)/shard_map/ppermute | solution.py:12
  325.2 1.0 copy-start
  405.0 4.9 copy-start.2
  486.4 33.9 %collective-permute-start.20 = (bf16[1,512,256]{2,1,0:T(8,128)(2,1)S(1)}, bf16[1,512,256]{2,1,0:T(8,128)(2,1)S(1)}, u32[]{:S(2)}, u32[]{:S(2)}) collective-permute-start(bf16[1,512,256]{2,1,0:T(8,128)(2,1)S(1)} %collective-permute-done.18), channel_id=1, source_target_pairs={{0,1},{1,2},{2,3},{3,4},{4,5},{5,6},{6,7},{7,0},{8,9},{9,10},{10,1... | collective-permute-start | bytes 786440 | tf_op jit(solution)/shard_map/ppermute | solution.py:18
  538.6 28.9 %collective-permute-start.22 = (bf16[1,512,256]{2,1,0:T(8,128)(2,1)S(1)}, bf16[1,512,256]{2,1,0:T(8,128)(2,1)S(1)}, u32[]{:S(2)}, u32[]{:S(2)}) collective-permute-start(bf16[1,512,256]{2,1,0:T(8,128)(2,1)S(1)} %collective-permute-done.20), channel_id=1, source_target_pairs={{0,1},{1,2},{2,3},{3,4},{4,5},{5,6},{6,7},{7,0},{8,9},{9,10},{10,1... | collective-permute-start | bytes 786440 | tf_op jit(solution)/shard_map/ppermute | solution.py:18
where the time goes:
time: 596 us; the launch traced here: 588 us
  starting transfers between devices  186 us (31%)
  local copies, waits for them, and re-layouts  185 us (31%)
  waiting for transfers between devices  143 us (24%)
  matrix products  33.8 us (6%)
  other arithmetic  20.7 us (3%)
  between operations  19.6 us (3%)
    pad x8, local copies, waits for them, and re-layouts, diagonal_sums(): jnp.pad(products.reshape(count, taps * columns), ((0, 0), (0, taps)))  114 us
    ppermute x14, waiting for transfers between devices, passed_along(): return lax.ppermute(value, axis, pairs)  108 us
    ppermute x14, starting transfers between devices, passed_along(): return lax.ppermute(value, axis, pairs)  95.5 us
    ppermute x9, starting transfers between devices, shifted(): lax.ppermute(value, axis, [(source, source + steps) for source in range(l...  61.3 us
    ppermute x9, waiting for transfers between devices, shifted(): lax.ppermute(value, axis, [(source, source + steps) for source in range(l...  35.4 us
    unnamed x24, local copies, waits for them, and re-layouts  24.1 us
    reshape x8, local copies, waits for them, and re-layouts, diagonal_sums(): skewed = flattened.reshape(count, taps, columns + 1)[:, :, :length]  21.2 us
    dot_general x8, matrix products, body(): jnp.einsum('kql,kqw->klw', block_now, window_rows, preferred_element_type...  20.3 us
  transfers between devices with their start and end apart: 25, of which 13 were waited for; matrix products, arithmetic and copies ran while one was open for 31% of the time, Pallas kernels for 0%

commit v1 on v0

v1 whole, which is shorter than its diff:
```python
import functools

import jax
import jax.numpy as jnp
from jax import lax
from jax.experimental import pallas as pl
from jax.experimental.pallas import tpu as pltpu
from jax.sharding import PartitionSpec as P

MESH = pl.DeviceIdType.MESH
F32 = jnp.float32
BF16 = jnp.bfloat16
I32 = jnp.int32
FOLD = 4
LANES = 128


def iota(shape, axis):
    return lax.broadcasted_iota(I32, shape, axis)


def log2(number):
    return number.bit_length() - 1


def kernel(
    chan_count, tmpl_count, run, width, per_group, chunks,
    raw_ref, ids_ref, tmpl_ref, off_ref, out_ref,
    snd1, rcv1, snd2, rcv2, rec, fol, bank, deep, weights, squares, prod, strips, norms, masks,
    s1, r1, s2, r2, st, rt, sz, rz, sf, rf, sr, rr, sq, rq, sn, rn, srf, rrf, sqf, rqf,
):
    rows, segment = raw_ref.shape
    span, taps = tmpl_ref.shape
    group_rows = per_group * width
    reach = span // group_rows
    links = reach // 2
    total_rows = (reach + 1) * group_rows
    pad_rows = deep.shape[0] // FOLD
    columns = deep.shape[1]
    lag = taps // FOLD
    homed = tmpl_count
    classes = chan_count // run
    block1 = run * width
    block2 = classes * width
    volume = float(span * taps)

    chan = lax.axis_index("chan")
    tmpl = lax.axis_index("tmpl")
    core = chan % 2
    place_z = (chan // 2) % run
    place_y = chan // (2 * run)
    my_class = place_y * 2 + core
    x_count = tmpl_count // 2
    partner = tmpl + 1 - 2 * (tmpl % 2)
    sibling = chan + 1 - 2 * core

    def chan_of(cls, z):
        return ((cls // 2) * run + z) * 2 + cls % 2

    def x_peer(step):
        return (tmpl + 2 * step) % tmpl_count

    behind = ((chan - 2 + chan_count) % chan_count, tmpl)
    ahead = ((chan + 2) % chan_count, tmpl)
    before = (chan, (tmpl - 1 + tmpl_count) % tmpl_count)
    after = (chan, (tmpl + 1) % tmpl_count)

    barrier = pltpu.get_barrier_semaphore()
    greeted = [(chan_of((my_class + d) % classes, place_z), tmpl) for d in range(1, classes)]
    greeted += [(chan_of(my_class, (place_z + d) % run), tmpl) for d in range(1, run)]
    greeted += [(chan, x_peer(d)) for d in range(1, x_count)]
    greeted += [(chan, partner), behind, ahead, before, after]
    for device in greeted:
        pl.semaphore_signal(barrier, inc=1, device_id=device, device_id_type=MESH)

    bank[tmpl, 0:span, :] = tmpl_ref[...]
    bank[tmpl, span:, :] = jnp.full((bank.shape[1] - span, taps), off_ref[0, 0].astype(F32)).astype(BF16)

    out_row = iota((rows, rows), 0)
    in_row = iota((rows, rows), 1)
    ids = ids_ref[...]
    cls = out_row >> log2(block1)
    dest_z = (out_row >> log2(width)) & (run - 1)
    dest = (((cls >> 1) * run + dest_z) << 1) + (cls & 1)
    same = (in_row & (width - 1)) == (out_row & (width - 1))
    select = ((ids >> log2(per_group)) == dest) & same
    places = jnp.sum(jnp.where(select, (ids & (per_group - 1)) + 1, 0).astype(F32), axis=1, keepdims=True)
    snd1[:, 0:segment] = jnp.dot(
        select.astype(F32).astype(BF16), raw_ref[...], preferred_element_type=F32
    ).astype(BF16)
    snd1[:, segment:] = jnp.broadcast_to(places, (rows, LANES)).astype(BF16)

    pl.semaphore_wait(barrier, len(greeted))

    sends = []

    def send(src, dst, s_sem, r_sem, device):
        copy = pltpu.make_async_remote_copy(
            src_ref=src, dst_ref=dst, send_sem=s_sem, recv_sem=r_sem, device_id=device, device_id_type=MESH
        )
        copy.start()
        sends.append(copy)
        return copy

    def block(index, size):
        return pl.ds(pl.multiple_of(index * size, size), size)

    first = []
    for d in range(1, classes):
        target = (my_class + d) % classes
        first.append(send(
            snd1.at[block(target, block1)], rcv1.at[block(my_class, block1)],
            s1.at[d], r1.at[d], (chan_of(target, place_z), tmpl),
        ))
    cuts = [span // chunks * part for part in range(chunks)] + [bank.shape[1]]
    to_partner = [
        send(bank.at[tmpl, cuts[p]:cuts[p + 1]], bank.at[tmpl, cuts[p]:cuts[p + 1]], sz.at[p], rz.at[p], (chan, partner))
        for p in range(chunks)
    ]
    to_peers = [
        send(bank.at[tmpl], bank.at[tmpl], st.at[d], rt.at[d], (chan, x_peer(d))) for d in range(1, x_count)
    ]
    rcv1[block(my_class, block1), :] = snd1[block(my_class, block1), :]

    pad = pad_rows - total_rows
    for s in range(FOLD):
        deep[s * pad_rows + total_rows:(s + 1) * pad_rows, :] = jnp.zeros((pad, columns), BF16)
    for s in range(2):
        squares[s * pad_rows + total_rows:(s + 1) * pad_rows, :] = jnp.zeros((pad, squares.shape[1]), BF16)

    for copy in first:
        copy.wait_recv()

    source = ((out_row >> log2(width)) & (classes - 1)) * block1 + (out_row >> log2(block2)) * width + (out_row & (width - 1))
    order = (in_row == source).astype(F32).astype(BF16)
    snd2[...] = jnp.dot(order, rcv1[...], preferred_element_type=F32).astype(BF16)
    second = []
    for d in range(1, run):
        target = (place_z + d) % run
        second.append(send(
            snd2.at[block(target, block2)], rcv2.at[block(place_z, block2)],
            s2.at[d], r2.at[d], (chan_of(my_class, target), tmpl),
        ))
    rcv2[block(place_z, block2), :] = snd2[block(place_z, block2), :]
    for copy in second:
        copy.wait_recv()
    arrived = rcv2[:, segment:segment + LANES].astype(F32)
    slot_row = iota((rows, LANES), 0)
    fiber_row = iota((rows, LANES), 1)
    pick = (arrived == ((fiber_row >> log2(width)) + 1).astype(F32)) & (
        (slot_row & (width - 1)) == (fiber_row & (width - 1))
    )
    pick = jnp.transpose(pick.astype(F32))[0:group_rows, :].astype(BF16)
    rec[0:group_rows, :] = jnp.dot(pick, rcv2[:, 0:segment], preferred_element_type=F32).astype(BF16)

    def prepare(index):
        template = bank[index, 0:span, :]
        offset = bank[index, span:span + 16, :].astype(F32)[0:1, 0:1].astype(I32)
        shape = (span, pad_rows)
        inside = chan + (iota(shape, 1) >> log2(group_rows)) < chan_count
        moved = ((iota(shape, 1) - iota(shape, 0)) == offset) & inside
        turned = lax.dot_general(
            template, moved.astype(F32).astype(BF16), (((0,), (0,)), ((), ())), preferred_element_type=F32
        ).astype(BF16)
        for s in range(FOLD):
            weights[block(index, lag), s * pad_rows:(s + 1) * pad_rows] = turned[s * lag:(s + 1) * lag, :]
        wide = template.astype(F32)
        norms[pl.ds(index, 1), :] = jnp.sum(wide * wide, axis=0, keepdims=True)
        lane = iota((1, pad_rows), 1)
        covered = (lane >= offset) & (lane < offset + span) & (chan + (lane >> log2(group_rows)) < chan_count)
        masks[pl.ds(index, 1), :] = covered.astype(F32)

    def group(index):
        return pl.ds(pl.multiple_of(index * group_rows, group_rows), group_rows)

    first_samples = send(rec.at[0:group_rows, 0:taps], fol.at[0:group_rows], sf, rf, before)
    relay, relay_fol, cross, cross_fol = [None], [None], [None], [None]

    def pass_on(step):
        relay.append(send(rec.at[group(2 * step - 2)], rec.at[group(2 * step)], sr.at[step], rr.at[step], behind))

    def pass_on_fol(step):
        relay_fol.append(send(fol.at[group(2 * step - 2)], fol.at[group(2 * step)], srf.at[step], rrf.at[step], behind))

    pass_on(1)
    prepare(tmpl)
    first_samples.wait_recv()
    pass_on_fol(1)
    forwards = []
    for step in range(1, links + 1):
        relay[step].wait_recv()
        if step < links:
            pass_on(step + 1)
        cross.append(send(
            rec.at[group(2 * (step - core))], rec.at[group(2 * step - 1)], sq.at[step], rq.at[step], (sibling, tmpl)
        ))
        relay_fol[step].wait_recv()
        if step < links:
            pass_on_fol(step + 1)
        cross_fol.append(send(
            fol.at[group(2 * (step - core))], fol.at[group(2 * step - 1)], sqf.at[step], rqf.at[step], (sibling, tmpl)
        ))
        for p in range(chunks * (step - 1) // links, chunks * step // links):
            to_partner[p].wait_recv()
            for d in range(1, x_count):
                forwards.append(send(
                    bank.at[partner, cuts[p]:cuts[p + 1]], bank.at[partner, cuts[p]:cuts[p + 1]],
                    sn.at[d, p], rn.at[d, p], (chan, x_peer(d)),
                ))
        if step < x_count:
            to_peers[step - 1].wait_recv()
            prepare((tmpl - 2 * step + tmpl_count) % tmpl_count)
    prepare(partner)
    for copy in cross[1:] + cross_fol[1:]:
        copy.wait_recv()

    last = tmpl == tmpl_count - 1

    def spread(index, carry):
        here = pl.ds(pl.multiple_of(index * group_rows, group_rows), group_rows)

        def below(s):
            return pl.ds(pl.multiple_of(index * group_rows + s * pad_rows, group_rows), group_rows)

        main = rec[here, :].astype(F32)
        tail = jnp.where(last, jnp.zeros((), F32), fol[here, :].astype(F32))
        whole = jnp.concatenate([main, tail], axis=1)
        narrow = whole.astype(BF16)
        turned = pltpu.roll(whole, whole.shape[1] - lag, 1).astype(BF16)
        for s in range(FOLD):
            side = turned if s * lag % LANES else narrow
            begin = (s * lag) // LANES * LANES
            deep[below(s), :] = side[:, begin:begin + columns]
        squared = whole * whole
        high = squared.astype(BF16)
        squares[below(0), :] = high
        squares[below(1), :] = (squared - high.astype(F32)).astype(BF16)
        return carry

    lax.fori_loop(0, reach + 1, spread, 0)

    for p in range(chunks):
        for d in range(1, x_count):
            forwards[p * (x_count - 1) + d - 1].wait_recv()
    for d in range(1, x_count):
        prepare((partner - 2 * d + tmpl_count) % tmpl_count)
    norm = jnp.sum(norms[...], axis=1, keepdims=True)

    mask = masks[...].astype(BF16)
    energy = jnp.dot(
        jnp.concatenate([mask, mask], axis=1), squares[...], preferred_element_type=F32
    )
    shift = 1
    while shift < taps:
        energy = energy + pltpu.roll(energy, energy.shape[1] - shift, 1)
        shift *= 2
    energy = energy[:, 0:segment]

    tile = 3 * LANES

    def multiply(index, carry):
        here = pl.ds(pl.multiple_of(index * tile, tile), tile)
        prod[:, here] = jnp.dot(weights[...], deep[:, here], preferred_element_type=F32)
        return carry

    lax.fori_loop(0, columns // tile, multiply, 0)

    def fold(index, carry):
        part = prod[pl.ds(pl.multiple_of(index * lag, lag), lag), :]
        half = lag // 2
        while half >= 8:
            part = part[0:half, :] + pltpu.roll(part[half:, :], columns - half, 1)
            half //= 2
        for t in range(columns // LANES):
            strips[t, pl.ds(pl.multiple_of(index * 8, 8), 8), :] = part[:, t * LANES:(t + 1) * LANES]
        return carry

    lax.fori_loop(0, homed, fold, 0)
    numer = jnp.zeros((homed, columns), F32)
    for a in range(8):
        strip = jnp.concatenate([strips[t, pl.ds(a, homed, stride=8), :] for t in range(columns // LANES)], axis=1)
        numer = numer + (strip if a == 0 else pltpu.roll(strip, columns - a, 1))
    out_ref[...] = numer[:, 0:segment] * jnp.sqrt(volume / (jnp.maximum(energy, volume) * norm))

    for copy in sends:
        copy.wait_send()


def body(run, raw_stretches, stretch_ids, templates, offsets):
    chan_count = lax.axis_size("chan")
    tmpl_count = lax.axis_size("tmpl")
    slots, width, segment = raw_stretches.shape
    span, taps = templates.shape[2:]
    per_group = chan_count // 2
    group_rows = per_group * width
    reach = span // group_rows
    links = reach // 2
    rows = slots * width
    total_rows = (reach + 1) * group_rows
    pad_rows = -(-total_rows // LANES) * LANES
    lag = taps // FOLD
    columns = -(-(segment + lag) // (3 * LANES)) * 3 * LANES
    classes = chan_count // run
    x_count = tmpl_count // 2
    chunks = 4
    homed = tmpl_count
    dma = pltpu.SemaphoreType.DMA
    vmem = pl.BlockSpec(memory_space=pltpu.VMEM)
    pairs = [dma((classes,))] * 2 + [dma((run,))] * 2 + [dma((x_count,))] * 2 + [dma((chunks,))] * 2 + [dma] * 2
    pairs += [dma((links + 1,))] * 4 + [dma((x_count, chunks))] * 2 + [dma((links + 1,))] * 4
    detection = pl.pallas_call(
        functools.partial(kernel, chan_count, tmpl_count, run, width, per_group, chunks),
        out_shape=jax.ShapeDtypeStruct((homed, segment), F32),
        in_specs=[vmem, vmem, vmem, pl.BlockSpec(memory_space=pltpu.SMEM)],
        out_specs=vmem,
        scratch_shapes=[
            pltpu.VMEM((rows, segment + LANES), BF16),
            pltpu.VMEM((rows, segment + LANES), BF16),
            pltpu.VMEM((rows, segment + LANES), BF16),
            pltpu.VMEM((rows, segment + LANES), BF16),
            pltpu.VMEM((total_rows, segment), BF16),
            pltpu.VMEM((total_rows, taps), BF16),
            pltpu.VMEM((homed, span + 16, taps), BF16),
            pltpu.VMEM((FOLD * pad_rows, columns), BF16),
            pltpu.VMEM((homed * lag, FOLD * pad_rows), BF16),
            pltpu.VMEM((2 * pad_rows, segment + taps), BF16),
            pltpu.VMEM((homed * lag, columns), F32),
            pltpu.VMEM((columns // LANES, homed * 8, LANES), F32),
            pltpu.VMEM((homed, taps), F32),
            pltpu.VMEM((homed, pad_rows), F32),
            *pairs,
        ],
        compiler_params=pltpu.CompilerParams(
            collective_id=0, has_side_effects=True, vmem_limit_bytes=48 * 1024 * 1024
        ),
    )(
        raw_stretches.reshape(rows, segment),
        jnp.repeat(stretch_ids, width).reshape(1, rows),
        templates.reshape(span, taps),
        offsets,
    )
    return detection.reshape(1, homed, segment)


def solution(mesh, run=8):
    placed = (P("chan", None, "tmpl"), P("chan"), P("chan", "tmpl", None, None), P("chan", "tmpl"))
    return jax.shard_map(
        functools.partial(body, run), mesh=mesh, in_specs=placed, out_specs=P("chan", None, "tmpl"), check_vma=False
    )
```

time: 596 us -> 97.6 us (0.16)
  the two profiles are of different devices: /device:TPU:77 before, /device:TPU:392 now
where the time goes in v1:
time: 97.6 us; the launch traced here: 97.5 us
  Pallas kernels  94.2 us (97%)
  local copies, waits for them, and re-layouts  2.58 us (3%)
    pallas_call x1, Pallas kernels, body(): pl.pallas_call(functools.partial(kernel, chan_count, tmpl_count, run, wid...  94.2 us

profile of v1, /device:TPU:392, one launch (start us, length us, event | category | flops | bytes accessed | tf_op | source)
XLA Modules:
  0.0 97.5 jit_solution(17171715145089585472)
XLA Ops:
  0.7 0.0 copy-start.1
  0.7 0.6 copy-done.1
  1.3 0.1 broadcast_in_dim.3
  1.4 0.1 reshape_reshape.3.ids_ref
  1.5 0.0 copy-start
  1.5 1.1 %reshape.9.raw_ref = bf16[128,1024]{1,0:T(8,128)(2,1)S(1)} reshape(bf16[64,2,1024]{2,1,0:T(2,128)(2,1)} %param.4) | data formatting | bytes 524288 | tf_op jit(solution)/shard_map/reshape | solution.py:337
  2.6 0.0 copy-done
  2.6 94.2 %shard_map.46 = f32[8,1024]{1,0:T(8,128)S(1)} custom-call(bf16[128,1024]{1,0:T(8,128)(2,1)S(1)} %reshape.9.raw_ref, s32[1,128]{1,0:T(1,128)S(1)} %reshape_reshape.3.ids_ref, bf16[512,256]{1,0:T(8,128)(2,1)S(1)} %bitcast.2, s32[1,1]{1,0:T(1,128)S(6)} %copy.6.off_ref), custom_call_target="tpu_custom_call" | custom-call | tf_op jit(solution)/shard_map/pallas_call | solution.py:311
  96.9 0.6 copy.7
Async XLA Ops:
  0.7 0.7 copy-start.1
  1.5 1.1 %copy-start = (bf16[1,1,512,256]{3,2,1,0:T(8,128)(2,1)S(1)}, bf16[1,1,512,256]{3,2,1,0:T(8,128)(2,1)}, u32[]{:S(2)}) copy-start(bf16[1,1,512,256]{3,2,1,0:T(8,128)(2,1)} %param.6) | copy-start | bytes 786436

commit v2 on v1

v2 whole, which is shorter than its diff:
```python
import functools

import jax
import jax.numpy as jnp
from jax import lax
from jax.experimental import pallas as pl
from jax.experimental.pallas import tpu as pltpu
from jax.sharding import PartitionSpec as P

MESH = pl.DeviceIdType.MESH
F32 = jnp.float32
BF16 = jnp.bfloat16
I32 = jnp.int32
FOLD = 2
LANES = 128


def iota(shape, axis):
    return lax.broadcasted_iota(I32, shape, axis)


def log2(number):
    return number.bit_length() - 1


def kernel(
    chan_count, tmpl_count, run, width, per_group,
    raw_ref, ids_ref, tmpl_ref, off_ref, out_ref,
    snd1, rcv1, snd2, rcv2, rec, bank, weights, squares, prod, strips, norms, masks, given, taken,
    s1, r1, s2, r2, st, rt, sd, rd, su, ru, scd, rcd, scu, rcu, sfe, rfe, sfo, rfo, so, ro,
):
    rows, segment = raw_ref.shape
    span, taps = tmpl_ref.shape
    group_rows = per_group * width
    reach = span // group_rows
    links = reach // 2
    total_rows = (reach + 1) * group_rows
    columns = prod.shape[1]
    lag = taps // FOLD
    x_count = tmpl_count // 2
    classes = chan_count // run
    block1 = run * width
    block2 = classes * width
    cut = segment // 2
    volume = float(span * taps)

    chan = lax.axis_index("chan")
    tmpl = lax.axis_index("tmpl")
    core = chan % 2
    place_z = (chan // 2) % run
    place_y = chan // (2 * run)
    place_x = tmpl // 2
    half = tmpl % 2
    my_class = place_y * 2 + core
    ring = place_z + run * half
    sibling = chan + 1 - 2 * core

    def chan_of(cls, z):
        return ((cls // 2) * run + z) * 2 + cls % 2

    def half_at(place):
        return ((place + 4 * run) % (2 * run)) // run

    def x_peer(step):
        return (tmpl + 2 * step + tmpl_count) % tmpl_count

    def near(steps, move):
        return ((chan + 2 * steps + 2 * chan_count) % chan_count, place_x * 2 + half_at(ring + move))

    parents = (
        {
            ("D", 1): ("D", 0), ("D", 3): ("D", 0), ("U", 2): ("D", 0), ("D", 2): ("D", 1), ("D", 4): ("D", 3),
            ("U", 4): ("U", 2), ("U", 0): ("U", 2), ("U", 3): ("U", 2), ("U", 1): ("U", 2),
        },
        {
            ("D", 1): ("D", 0), ("D", 3): ("D", 0), ("U", 3): ("D", 0), ("D", 2): ("D", 1), ("D", 4): ("D", 3),
            ("U", 0): ("U", 3), ("U", 1): ("U", 3), ("U", 2): ("U", 3), ("U", 4): ("U", 3),
        },
    )

    def route(node, parent):
        return parent[1] - node[1], parent[1] - node[1] + (run if node[0] != parent[0] else 0)

    partner = (chan, tmpl + 1 - 2 * half)
    earlier, earlier_sibling = (chan, x_peer(-1)), (sibling, x_peer(-1))

    barrier = pltpu.get_barrier_semaphore()
    greeted = [(chan_of((my_class + d) % classes, place_z), tmpl) for d in range(1, classes)]
    greeted += [(chan_of(my_class, (place_z + d) % run), tmpl) for d in range(1, run)]
    greeted += [(chan, x_peer(d)) for d in range(1, x_count)]
    routes = {route(*link) for table in parents for link in table.items()}
    routes = sorted(routes | {(-steps, -move) for steps, move in routes})
    greeted += [near(steps, move) for steps, move in routes]
    greeted += [partner, earlier_sibling, (sibling, x_peer(1))]
    for device in greeted:
        pl.semaphore_signal(barrier, inc=1, device_id=device, device_id_type=MESH)

    bank[place_x, 0:span, :] = tmpl_ref[...]
    bank[place_x, span:, :] = jnp.full((bank.shape[1] - span, taps), off_ref[0, 0].astype(F32)).astype(BF16)

    out_row = iota((rows, rows), 0)
    in_row = iota((rows, rows), 1)
    ids = ids_ref[...]
    cls = out_row >> log2(block1)
    dest_z = (out_row >> log2(width)) & (run - 1)
    dest = (((cls >> 1) * run + dest_z) << 1) + (cls & 1)
    same = (in_row & (width - 1)) == (out_row & (width - 1))
    select = ((ids >> log2(per_group)) == dest) & same
    places = jnp.sum(jnp.where(select, (ids & (per_group - 1)) + 1, 0).astype(F32), axis=1, keepdims=True)
    snd1[:, LANES:] = jnp.dot(
        select.astype(F32).astype(BF16), raw_ref[...], preferred_element_type=F32
    ).astype(BF16)
    snd1[:, 0:LANES] = jnp.broadcast_to(places, (rows, LANES)).astype(BF16)

    pl.semaphore_wait(barrier, len(greeted))

    sends = []

    def copy_to(src, dst, s_sem, r_sem, device):
        return pltpu.make_async_remote_copy(
            src_ref=src, dst_ref=dst, send_sem=s_sem, recv_sem=r_sem, device_id=device, device_id_type=MESH
        )

    def send(*args):
        copy = copy_to(*args)
        copy.start()
        sends.append(copy)
        return copy

    def block(index, size):
        return pl.ds(pl.multiple_of(index * size, size), size)

    stretches = (pl.ds(0, LANES + cut), pl.ds(LANES + cut, segment - cut))
    first = [[], []]
    for h, lanes in enumerate(stretches):
        for d in range(1, classes):
            target = (my_class + d) % classes
            first[h].append(send(
                snd1.at[block(target, block1), lanes], rcv1.at[block(my_class, block1), lanes],
                s1.at[d, h], r1.at[d, h], (chan_of(target, place_z), tmpl),
            ))
    to_peers = [
        send(bank.at[place_x], bank.at[place_x], st.at[d], rt.at[d], (chan, x_peer(d))) for d in range(1, x_count)
    ]
    rcv1[block(my_class, block1), :] = snd1[block(my_class, block1), :]

    source = ((out_row >> log2(width)) & (classes - 1)) * block1 + (out_row >> log2(block2)) * width + (out_row & (width - 1))
    order = (in_row == source).astype(F32).astype(BF16)
    second = [[], []]
    for h, lanes in enumerate(stretches):
        for copy in first[h]:
            copy.wait_recv()
        snd2[:, lanes] = jnp.dot(order, rcv1[:, lanes], preferred_element_type=F32).astype(BF16)
        for d in range(1, run):
            target = (place_z + d) % run
            second[h].append(send(
                snd2.at[block(target, block2), lanes], rcv2.at[block(place_z, block2), lanes],
                s2.at[d, h], r2.at[d, h], (chan_of(my_class, target), tmpl),
            ))
    rcv2[block(place_z, block2), :] = snd2[block(place_z, block2), :]

    def prepare(index):
        template = bank[index, 0:span, :]
        offset = bank[index, span:span + 16, :].astype(F32)[0:1, 0:1].astype(I32)
        shape = (span, total_rows)
        inside = chan + (iota(shape, 1) >> log2(group_rows)) < chan_count
        moved = ((iota(shape, 1) - iota(shape, 0)) == offset) & inside
        turned = lax.dot_general(
            template, moved.astype(F32).astype(BF16), (((0,), (0,)), ((), ())), preferred_element_type=F32
        ).astype(BF16)
        for s in range(FOLD):
            weights[s, block(index, lag), :] = turned[s * lag:(s + 1) * lag, :]
        wide = template.astype(F32)
        norms[pl.ds(index, 1), :] = jnp.sum(wide * wide, axis=0, keepdims=True)
        lane = iota((1, total_rows), 1)
        covered = (lane >= offset) & (lane < offset + span) & (chan + (lane >> log2(group_rows)) < chan_count)
        masks[pl.ds(index, 1), :] = covered.astype(F32)

    def group(index):
        return pl.ds(pl.multiple_of(index * group_rows, group_rows), group_rows)

    whole_down = ((0, cut), (cut, segment - cut))
    arrivals = {}

    def lanes_of(which, p):
        return pl.ds(pl.multiple_of(which * segment + whole_down[p][0], LANES), whole_down[p][1])

    def which_of(kind, j):
        near_half = half_at(ring + j)
        return near_half if kind == "D" else 1 - near_half

    def pass_on(parent, p):
        for node in parents[p]:
            if parents[p][node] == parent:
                (kind, j), lanes = node, lanes_of(which_of(*parent), p)
                s_sem, r_sem = {"D": (sd, rd), "U": (su, ru)}[kind]
                arrivals[kind, j, p] = send(
                    rec.at[group(2 * parent[1]), lanes], rec.at[group(2 * j), lanes], s_sem.at[j, p], r_sem.at[j, p],
                    near(*route(node, parent)),
                )

    def cross(t, kind, p):
        j = t - core
        lanes = lanes_of(which_of(kind, j), p)
        s_sem, r_sem = {"D": (scd, rcd), "U": (scu, rcu)}[kind]
        return copy_to(
            rec.at[group(2 * j), lanes], rec.at[group(2 * t - 1), lanes], s_sem.at[t, p], r_sem.at[t, p],
            (sibling, tmpl),
        )

    tail = pl.ds(2 * segment, taps)

    def lend(j):
        return copy_to(rec.at[group(2 * j), 0:taps], rec.at[group(2 * j), tail], sfe.at[j], rfe.at[j], earlier)

    def lend_cross(t):
        return copy_to(
            rec.at[group(2 * (t - core)), 0:taps], rec.at[group(2 * t - 1), tail], sfo.at[t], rfo.at[t],
            earlier_sibling,
        )

    def share(j, kind, p):
        which = which_of(kind, j)
        t = j + core
        inner = 1 <= j < links
        if inner:
            cross(t, kind, p).start()
        else:
            @pl.when(core == (1 if j == 0 else 0))
            def _():
                cross(t, kind, p).start()

        if p == 0:
            @pl.when(which == 0)
            def _():
                lend(j).start()
                if inner:
                    lend_cross(t).start()

            if not inner:
                @pl.when((which == 0) & (core == (1 if j == 0 else 0)))
                def _():
                    lend_cross(t).start()

    last = place_x == x_count - 1

    def square(index, lanes):
        value = rec[group(index), lanes].astype(F32)
        squared = value * value
        high = squared.astype(BF16)
        squares[0, group(index), lanes] = high
        squares[1, group(index), lanes] = (squared - high.astype(F32)).astype(BF16)

    def square_tail(index):
        @pl.when(last)
        def _():
            rec[group(index), tail] = jnp.zeros((group_rows, taps), BF16)

        square(index, tail)

    def finish_odd(t, kind):
        for p in range(2):
            copy = cross(t, kind, p)
            copy.wait_recv()
            square(2 * t - 1, lanes_of(which_of(kind, t - 1 + core), p))

    def finish_lent(j):
        lend(j).wait_recv()
        square_tail(2 * j)
        if j > 0:
            lend_cross(j).wait_recv()
            square_tail(2 * j - 1)

    prepare(place_x)
    arrived_rows = iota((rows, LANES), 0)
    fiber_row = iota((rows, LANES), 1)
    same_channel = (arrived_rows & (width - 1)) == (fiber_row & (width - 1))
    wanted = ((fiber_row >> log2(width)) + 1).astype(F32)
    for h in range(2):
        for copy in second[h]:
            copy.wait_recv()
        if h == 0:
            pick = (rcv2[:, 0:LANES].astype(F32) == wanted) & same_channel
            pick = jnp.transpose(pick.astype(F32))[0:group_rows, :].astype(BF16)
        begin, size = whole_down[h]
        rec[0:group_rows, lanes_of(half, h)] = jnp.dot(
            pick, rcv2[:, LANES + begin:LANES + begin + size], preferred_element_type=F32
        ).astype(BF16)
        pass_on(("D", 0), h)
        share(0, "D", h)
        square(0, lanes_of(half, h))
        if h == 0:
            to_peers[0].wait_recv()
            prepare((place_x - 1 + x_count) % x_count)

    def came(kind, j, p):
        arrivals[kind, j, p].wait_recv()
        pass_on((kind, j), p)
        share(j, kind, p)
        square(2 * j, lanes_of(which_of(kind, j), p))

    due = (
        {
            ("D", 1): 3, ("D", 3): 6, ("D", 2): 7, ("D", 4): 10, ("U", 2): 12,
            ("U", 3): 17, ("U", 1): 18, ("U", 4): 19, ("U", 0): 20,
        },
        {
            ("D", 1): 9, ("D", 3): 11, ("D", 2): 14, ("D", 4): 15, ("U", 3): 18,
            ("U", 4): 23, ("U", 2): 24, ("U", 1): 25, ("U", 0): 26,
        },
    )
    events = sorted((due[p][node], *node, p) for p in range(2) for node in parents[p])
    for count, (_, kind, j, p) in enumerate(events):
        came(kind, j, p)
        if 1 <= count < x_count - 1:
            to_peers[count].wait_recv()
            prepare((place_x - 1 - count + x_count) % x_count)
        if (kind, j, p) == ("U", 3, 1):
            for t in range(1, links + 1):
                finish_odd(t, "D")
    for t in range(1, links + 1):
        finish_odd(t, "U")
    for j in range(links, -1, -1):
        finish_lent(j)

    norm = jnp.sum(norms[...], axis=1, keepdims=True)
    mask = masks[...].astype(BF16)
    tile = LANES * (1 if columns % (3 * LANES) else 3)

    def score(which):
        def multiply(index, carry):
            here = pl.ds(pl.multiple_of(index * tile, tile), tile)
            there = pl.ds(pl.multiple_of(which * segment + index * tile, LANES), tile)
            total = jnp.dot(weights[0], rec[:, there], preferred_element_type=F32)
            for s in range(1, FOLD):
                there = pl.ds(pl.multiple_of(which * segment + index * tile + s * lag, LANES), tile)
                total = total + jnp.dot(weights[s], rec[:, there], preferred_element_type=F32)
            prod[:, here] = total
            return carry

        lax.fori_loop(0, columns // tile, multiply, 0)
        there = pl.ds(pl.multiple_of(which * segment, LANES), segment + taps)
        energy = jnp.dot(mask, squares[0, :, there], preferred_element_type=F32)
        energy = energy + jnp.dot(mask, squares[1, :, there], preferred_element_type=F32)
        shift = 1
        while shift < taps:
            energy = energy + pltpu.roll(energy, energy.shape[1] - shift, 1)
            shift *= 2
        energy = energy[:, 0:segment]

        def fold(index, carry):
            part = prod[pl.ds(pl.multiple_of(index * lag, lag), lag), :]
            size = lag // 2
            while size >= 8:
                part = part[0:size, :] + pltpu.roll(part[size:, :], columns - size, 1)
                size //= 2
            for t in range(columns // LANES):
                strips[t, pl.ds(pl.multiple_of(index * 8, 8), 8), :] = part[:, t * LANES:(t + 1) * LANES]
            return carry

        lax.fori_loop(0, x_count, fold, 0)
        numer = jnp.zeros((x_count, columns), F32)
        for a in range(8):
            strip = jnp.concatenate(
                [strips[t, pl.ds(a, x_count, stride=8), :] for t in range(columns // LANES)], axis=1
            )
            numer = numer + (strip if a == 0 else pltpu.roll(strip, columns - a, 1))
        return numer[:, 0:segment] * jnp.sqrt(volume / (jnp.maximum(energy, volume) * norm))

    given[...] = score(1 - half)
    trade = send(given, taken, so, ro, partner)
    own = score(half)
    for x in range(x_count):
        out_ref[pl.ds(2 * x + half, 1), :] = own[x:x + 1, :]
    trade.wait_recv()
    for x in range(x_count):
        out_ref[pl.ds(2 * x + 1 - half, 1), :] = taken[x:x + 1, :]

    for copy in sends:
        copy.wait_send()
    for t in range(1, links + 1):
        for kind in ("D", "U"):
            for p in range(2):
                cross(t, kind, p).wait_send()
        lend_cross(t).wait_send()
    for j in range(links + 1):
        lend(j).wait_send()


def body(run, raw_stretches, stretch_ids, templates, offsets):
    chan_count = lax.axis_size("chan")
    tmpl_count = lax.axis_size("tmpl")
    slots, width, segment = raw_stretches.shape
    span, taps = templates.shape[2:]
    per_group = chan_count // 2
    group_rows = per_group * width
    reach = span // group_rows
    links = reach // 2
    rows = slots * width
    total_rows = (reach + 1) * group_rows
    lag = taps // FOLD
    columns = segment + lag
    classes = chan_count // run
    x_count = tmpl_count // 2
    homed = tmpl_count
    dma = pltpu.SemaphoreType.DMA
    vmem = pl.BlockSpec(memory_space=pltpu.VMEM)
    pairs = [dma((classes, 2))] * 2 + [dma((run, 2))] * 2 + [dma((x_count,))] * 2
    pairs += [dma((links + 1, 2))] * 8 + [dma((links + 1,))] * 4 + [dma] * 2
    detection = pl.pallas_call(
        functools.partial(kernel, chan_count, tmpl_count, run, width, per_group),
        out_shape=jax.ShapeDtypeStruct((homed, segment), F32),
        in_specs=[vmem, vmem, vmem, pl.BlockSpec(memory_space=pltpu.SMEM)],
        out_specs=vmem,
        scratch_shapes=[
            pltpu.VMEM((rows, segment + LANES), BF16),
            pltpu.VMEM((rows, segment + LANES), BF16),
            pltpu.VMEM((rows, segment + LANES), BF16),
            pltpu.VMEM((rows, segment + LANES), BF16),
            pltpu.VMEM((total_rows, 2 * segment + taps), BF16),
            pltpu.VMEM((x_count, span + 16, taps), BF16),
            pltpu.VMEM((FOLD, x_count * lag, total_rows), BF16),
            pltpu.VMEM((2, total_rows, 2 * segment + taps), BF16),
            pltpu.VMEM((x_count * lag, columns), F32),
            pltpu.VMEM((columns // LANES, x_count * 8, LANES), F32),
            pltpu.VMEM((x_count, taps), F32),
            pltpu.VMEM((x_count, total_rows), F32),
            pltpu.VMEM((x_count, segment), F32),
            pltpu.VMEM((x_count, segment), F32),
            *pairs,
        ],
        compiler_params=pltpu.CompilerParams(
            collective_id=0, has_side_effects=True, vmem_limit_bytes=48 * 1024 * 1024
        ),
    )(
        raw_stretches.reshape(rows, segment),
        jnp.repeat(stretch_ids, width).reshape(1, rows),
        templates.reshape(span, taps),
        offsets,
    )
    return detection.reshape(1, homed, segment)


def solution(mesh, run=8):
    placed = (P("chan", None, "tmpl"), P("chan"), P("chan", "tmpl", None, None), P("chan", "tmpl"))
    return jax.shard_map(
        functools.partial(body, run), mesh=mesh, in_specs=placed, out_specs=P("chan", None, "tmpl"), check_vma=False
    )
```

time: 97.6 us -> 89.8 us (0.920)
  the two profiles are of different devices: /device:TPU:392 before, /device:TPU:1 now
where the time goes in v2:
time: 89.8 us; the launch traced here: 89.7 us
  Pallas kernels  86.4 us (96%)
  local copies, waits for them, and re-layouts  2.58 us (3%)
    pallas_call x1, Pallas kernels, body(): pl.pallas_call(functools.partial(kernel, chan_count, tmpl_count, run, wid...  86.4 us

profile of v2, /device:TPU:1, one launch (start us, length us, event | category | flops | bytes accessed | tf_op | source)
XLA Modules:
  0.0 89.7 jit_solution(10140424454653512432)
XLA Ops:
  0.7 0.0 copy-start.1
  0.7 0.6 copy-done.1
  1.3 0.1 broadcast_in_dim.3
  1.4 0.1 reshape_reshape.3.ids_ref
  1.5 0.0 copy-start
  1.5 1.1 %reshape.9.raw_ref = bf16[128,1024]{1,0:T(8,128)(2,1)S(1)} reshape(bf16[64,2,1024]{2,1,0:T(2,128)(2,1)} %param.4) | data formatting | bytes 524288 | tf_op jit(solution)/shard_map/reshape | solution.py:436
  2.6 0.0 copy-done
  2.6 86.4 %shard_map.46 = f32[8,1024]{1,0:T(8,128)S(1)} custom-call(bf16[128,1024]{1,0:T(8,128)(2,1)S(1)} %reshape.9.raw_ref, s32[1,128]{1,0:T(1,128)S(1)} %reshape_reshape.3.ids_ref, bf16[512,256]{1,0:T(8,128)(2,1)S(1)} %bitcast.2, s32[1,1]{1,0:T(1,128)S(6)} %copy.6.off_ref), custom_call_target="tpu_custom_call" | custom-call | tf_op jit(solution)/shard_map/pallas_call | solution.py:410
  89.0 0.6 copy.7
Async XLA Ops:
  0.7 0.7 copy-start.1
  1.5 1.1 %copy-start = (bf16[1,1,512,256]{3,2,1,0:T(8,128)(2,1)S(1)}, bf16[1,1,512,256]{3,2,1,0:T(8,128)(2,1)}, u32[]{:S(2)}) copy-start(bf16[1,1,512,256]{3,2,1,0:T(8,128)(2,1)} %param.6) | copy-start | bytes 786436

commit v3 on v2

--- a/solution.py
+++ b/solution.py
@@ -69,12 +69,12 @@
 
     parents = (
         {
-            ("D", 1): ("D", 0), ("D", 3): ("D", 0), ("U", 2): ("D", 0), ("D", 2): ("D", 1), ("D", 4): ("D", 3),
-            ("U", 4): ("U", 2), ("U", 0): ("U", 2), ("U", 3): ("U", 2), ("U", 1): ("U", 2),
+            ("D", 1): ("D", 0), ("D", 2): ("D", 0), ("D", 3): ("D", 2), ("D", 4): ("D", 2), ("U", 2): ("D", 0),
+            ("U", 1): ("U", 2), ("U", 3): ("U", 2), ("U", 0): ("U", 1), ("U", 4): ("U", 3),
         },
         {
-            ("D", 1): ("D", 0), ("D", 3): ("D", 0), ("U", 3): ("D", 0), ("D", 2): ("D", 1), ("D", 4): ("D", 3),
-            ("U", 0): ("U", 3), ("U", 1): ("U", 3), ("U", 2): ("U", 3), ("U", 4): ("U", 3),
+            ("D", 1): ("D", 0), ("D", 2): ("D", 0), ("D", 3): ("D", 2), ("D", 4): ("D", 2), ("U", 2): ("D", 0),
+            ("U", 4): ("U", 2), ("U", 0): ("U", 2), ("U", 3): ("U", 2), ("U", 1): ("U", 2),
         },
     )
 
@@ -301,12 +301,12 @@
 
     due = (
         {
-            ("D", 1): 3, ("D", 3): 6, ("D", 2): 7, ("D", 4): 10, ("U", 2): 12,
-            ("U", 3): 17, ("U", 1): 18, ("U", 4): 19, ("U", 0): 20,
+            ("D", 1): 4, ("D", 2): 5, ("D", 3): 10, ("D", 4): 11, ("U", 2): 10,
+            ("U", 1): 14, ("U", 3): 15, ("U", 0): 18, ("U", 4): 19,
         },
         {
-            ("D", 1): 9, ("D", 3): 11, ("D", 2): 14, ("D", 4): 15, ("U", 3): 18,
-            ("U", 4): 23, ("U", 2): 24, ("U", 1): 25, ("U", 0): 26,
+            ("D", 1): 11, ("D", 2): 12, ("D", 3): 16, ("D", 4): 17, ("U", 2): 17,
+            ("U", 1): 21, ("U", 3): 22, ("U", 0): 23, ("U", 4): 24,
         },
     )
     events = sorted((due[p][node], *node, p) for p in range(2) for node in parents[p])
@@ -315,7 +315,7 @@
         if 1 <= count < x_count - 1:
             to_peers[count].wait_recv()
             prepare((place_x - 1 - count + x_count) % x_count)
-        if (kind, j, p) == ("U", 3, 1):
+        if (kind, j, p) == ("D", links, 1):
             for t in range(1, links + 1):
                 finish_odd(t, "D")
     for t in range(1, links + 1):

time: 89.8 us -> 88.4 us (0.984)
  Pallas kernels: 86.4 us -> 84.2 us
    pallas_call x1, Pallas kernels: 86.4 us -> 84.2 us  [body(): pl.pallas_call(functools.partial(kernel, chan_count, tmpl_count, run, wid...]
where the time goes in v3:
time: 88.4 us; the launch traced here: 87.5 us
  Pallas kernels  84.2 us (95%)
  local copies, waits for them, and re-layouts  2.58 us (3%)
    pallas_call x1, Pallas kernels, body(): pl.pallas_call(functools.partial(kernel, chan_count, tmpl_count, run, wid...  84.2 us

profile of v3, /device:TPU:1, one launch (start us, length us, event | category | flops | bytes accessed | tf_op | source)
XLA Modules:
  0.0 87.5 jit_solution(677675728827927610)
XLA Ops:
  0.7 0.0 copy-start.1
  0.7 0.6 copy-done.1
  1.3 0.1 broadcast_in_dim.3
  1.4 0.1 reshape_reshape.3.ids_ref
  1.5 0.0 copy-start
  1.5 1.1 %reshape.9.raw_ref = bf16[128,1024]{1,0:T(8,128)(2,1)S(1)} reshape(bf16[64,2,1024]{2,1,0:T(2,128)(2,1)} %param.4) | data formatting | bytes 524288 | tf_op jit(solution)/shard_map/reshape | solution.py:436
  2.6 0.0 copy-done
  2.6 84.2 %shard_map.46 = f32[8,1024]{1,0:T(8,128)S(1)} custom-call(bf16[128,1024]{1,0:T(8,128)(2,1)S(1)} %reshape.9.raw_ref, s32[1,128]{1,0:T(1,128)S(1)} %reshape_reshape.3.ids_ref, bf16[512,256]{1,0:T(8,128)(2,1)S(1)} %bitcast.2, s32[1,1]{1,0:T(1,128)S(6)} %copy.6.off_ref), custom_call_target="tpu_custom_call" | custom-call | tf_op jit(solution)/shard_map/pallas_call | solution.py:410
  86.9 0.6 copy.7
Async XLA Ops:
  0.7 0.7 copy-start.1
  1.5 1.1 %copy-start = (bf16[1,1,512,256]{3,2,1,0:T(8,128)(2,1)S(1)}, bf16[1,1,512,256]{3,2,1,0:T(8,128)(2,1)}, u32[]{:S(2)}) copy-start(bf16[1,1,512,256]{3,2,1,0:T(8,128)(2,1)} %param.6) | copy-start | bytes 786436

commit v4 on v3

--- a/solution.py
+++ b/solution.py
@@ -100,13 +100,19 @@
 
     out_row = iota((rows, rows), 0)
     in_row = iota((rows, rows), 1)
-    ids = ids_ref[...]
+    slots = rows // width
+    ids = jnp.broadcast_to(ids_ref[...], (8, slots))
+    parts = jnp.where(iota((8, slots), 0) == 0, ids >> log2(per_group), ids & (per_group - 1))
+    spread = iota((slots, rows), 0) == (iota((slots, rows), 1) >> log2(width))
+    parts = jnp.dot(
+        parts.astype(F32).astype(BF16), spread.astype(F32).astype(BF16), preferred_element_type=F32
+    ).astype(I32)
     cls = out_row >> log2(block1)
     dest_z = (out_row >> log2(width)) & (run - 1)
     dest = (((cls >> 1) * run + dest_z) << 1) + (cls & 1)
     same = (in_row & (width - 1)) == (out_row & (width - 1))
-    select = ((ids >> log2(per_group)) == dest) & same
-    places = jnp.sum(jnp.where(select, (ids & (per_group - 1)) + 1, 0).astype(F32), axis=1, keepdims=True)
+    select = (parts[0:1, :] == dest) & same
+    places = jnp.sum(jnp.where(select, parts[1:2, :] + 1, 0).astype(F32), axis=1, keepdims=True)
     snd1[:, LANES:] = jnp.dot(
         select.astype(F32).astype(BF16), raw_ref[...], preferred_element_type=F32
     ).astype(BF16)
@@ -434,7 +440,7 @@
         ),
     )(
         raw_stretches.reshape(rows, segment),
-        jnp.repeat(stretch_ids, width).reshape(1, rows),
+        stretch_ids.reshape(1, slots),
         templates.reshape(span, taps),
         offsets,
     )

time: 88.4 us -> 87.6 us (level)
  no operation moved by 1% of the time
where the time goes in v4:
time: 87.6 us; the launch traced here: 86.6 us
  Pallas kernels  84.2 us (96%)
  local copies, waits for them, and re-layouts  1.72 us (2%)
    pallas_call x1, Pallas kernels, body(): pl.pallas_call(functools.partial(kernel, chan_count, tmpl_count, run, wid...  84.2 us

profile of v4, /device:TPU:1, one launch (start us, length us, event | category | flops | bytes accessed | tf_op | source)
XLA Modules:
  0.0 86.6 jit_solution(9760026257934949550)
XLA Ops:
  0.7 0.0 copy-start
  0.7 0.0 copy-start.1
  0.7 1.1 %reshape.12.raw_ref = bf16[128,1024]{1,0:T(8,128)(2,1)S(1)} reshape(bf16[64,2,1024]{2,1,0:T(2,128)(2,1)} %param.4) | data formatting | bytes 524288 | tf_op jit(solution)/shard_map/reshape | solution.py:442
  1.8 0.0 copy-done
  1.8 0.0 copy-done.1
  1.8 84.2 %shard_map.46 = f32[8,1024]{1,0:T(8,128)S(1)} custom-call(bf16[128,1024]{1,0:T(8,128)(2,1)S(1)} %reshape.12.raw_ref, s32[1,64]{1,0:T(1,128)S(1)} %bitcast.5, bf16[512,256]{1,0:T(8,128)(2,1)S(1)} %bitcast.3, s32[1,1]{1,0:T(1,128)S(6)} %copy.6.off_ref), custom_call_target="tpu_custom_call" | custom-call | tf_op jit(solution)/shard_map/pallas_call | solution.py:416
  86.0 0.6 copy.7
Async XLA Ops:
  0.7 1.1 %copy-start = (bf16[1,1,512,256]{3,2,1,0:T(8,128)(2,1)S(1)}, bf16[1,1,512,256]{3,2,1,0:T(8,128)(2,1)}, u32[]{:S(2)}) copy-start(bf16[1,1,512,256]{3,2,1,0:T(8,128)(2,1)} %param.6) | copy-start | bytes 786436
  0.7 1.1 %copy-start.1 = (s32[64]{0:T(128)S(1)}, s32[64]{0:T(128)}, u32[]{:S(2)}) copy-start(s32[64]{0:T(128)} %param.5) | copy-start | bytes 772

commit v5 on v4

--- a/solution.py
+++ b/solution.py
@@ -92,7 +92,7 @@
     routes = sorted(routes | {(-steps, -move) for steps, move in routes})
     greeted += [near(steps, move) for steps, move in routes]
     greeted += [partner, earlier_sibling, (sibling, x_peer(1))]
-    for device in greeted:
+    for device in reversed(greeted):
         pl.semaphore_signal(barrier, inc=1, device_id=device, device_id_type=MESH)
 
     bank[place_x, 0:span, :] = tmpl_ref[...]
@@ -145,9 +145,6 @@
                 snd1.at[block(target, block1), lanes], rcv1.at[block(my_class, block1), lanes],
                 s1.at[d, h], r1.at[d, h], (chan_of(target, place_z), tmpl),
             ))
-    to_peers = [
-        send(bank.at[place_x], bank.at[place_x], st.at[d], rt.at[d], (chan, x_peer(d))) for d in range(1, x_count)
-    ]
     rcv1[block(my_class, block1), :] = snd1[block(my_class, block1), :]
 
     source = ((out_row >> log2(width)) & (classes - 1)) * block1 + (out_row >> log2(block2)) * width + (out_row & (width - 1))
@@ -163,6 +160,9 @@
                 snd2.at[block(target, block2), lanes], rcv2.at[block(place_z, block2), lanes],
                 s2.at[d, h], r2.at[d, h], (chan_of(my_class, target), tmpl),
             ))
+    to_peers = [
+        send(bank.at[place_x], bank.at[place_x], st.at[d], rt.at[d], (chan, x_peer(d))) for d in range(1, x_count)
+    ]
     rcv2[block(place_z, block2), :] = snd2[block(place_z, block2), :]
 
     def prepare(index):

time: 87.6 us -> 86.9 us (level)
  no operation moved by 1% of the time
where the time goes in v5:
time: 86.9 us; the launch traced here: 86.8 us
  Pallas kernels  84.3 us (97%)
  local copies, waits for them, and re-layouts  1.72 us (2%)
    pallas_call x1, Pallas kernels, body(): pl.pallas_call(functools.partial(kernel, chan_count, tmpl_count, run, wid...  84.3 us

profile of v5, /device:TPU:1, one launch (start us, length us, event | category | flops | bytes accessed | tf_op | source)
XLA Modules:
  0.0 86.8 jit_solution(5574563276648051020)
XLA Ops:
  0.7 0.0 copy-start
  0.7 0.0 copy-start.1
  0.7 1.1 %reshape.12.raw_ref = bf16[128,1024]{1,0:T(8,128)(2,1)S(1)} reshape(bf16[64,2,1024]{2,1,0:T(2,128)(2,1)} %param.4) | data formatting | bytes 524288 | tf_op jit(solution)/shard_map/reshape | solution.py:442
  1.8 0.0 copy-done
  1.8 0.0 copy-done.1
  1.8 84.3 %shard_map.46 = f32[8,1024]{1,0:T(8,128)S(1)} custom-call(bf16[128,1024]{1,0:T(8,128)(2,1)S(1)} %reshape.12.raw_ref, s32[1,64]{1,0:T(1,128)S(1)} %bitcast.5, bf16[512,256]{1,0:T(8,128)(2,1)S(1)} %bitcast.3, s32[1,1]{1,0:T(1,128)S(6)} %copy.6.off_ref), custom_call_target="tpu_custom_call" | custom-call | tf_op jit(solution)/shard_map/pallas_call | solution.py:416
  86.1 0.6 copy.7
Async XLA Ops:
  0.7 1.1 %copy-start = (bf16[1,1,512,256]{3,2,1,0:T(8,128)(2,1)S(1)}, bf16[1,1,512,256]{3,2,1,0:T(8,128)(2,1)}, u32[]{:S(2)}) copy-start(bf16[1,1,512,256]{3,2,1,0:T(8,128)(2,1)} %param.6) | copy-start | bytes 786436
  0.7 1.1 %copy-start.1 = (s32[64]{0:T(128)S(1)}, s32[64]{0:T(128)}, u32[]{:S(2)}) copy-start(s32[64]{0:T(128)} %param.5) | copy-start | bytes 772
